TPU v7x, 256 devices: a whole 4x4x8 slice. The times are simulated.
256 devices in a mesh: tile: 64 (over y, z, core), band: 4 (over x).
Axes of the slice: x: 4, y: 4, z: 8, core: 2. Of those that a mesh axis runs over, the one named last changes fastest.
Arguments:
- params: float32 [2048, 44], P(('tile', 'band')), may hold values from -4 to 4
- offsets: int32 [2048, 2], P(('tile', 'band')), may hold values from -32 to 351
- counts: int32 [256], P(('tile', 'band')), may hold values from 1 to 8, 1153 in all
- image: float32 [64, 5, 384, 384], P('tile'), may hold values from 0.25 to 4
- background: float32 [64, 5], P('tile'), may hold values from 0.5 to 2
- psf_y: float32 [5, 25], replicated, may hold values from 0.02 to 0.1
- psf_x: float32 [5, 25], replicated, may hold values from 0.02 to 0.1
Outputs:
- gradient: float32 [2048, 44], P(('tile', 'band'))
All inputs are finite; a program needn't handle non-finite values. No bound on the sum of `counts` on one device may be relied on, other than what follows from the above.
Results may differ from a plain program's by a relative error of at most 0.0001.
Values sent between devices are 32-bit elements; how exact they have to be, the bound alone decides.
A program may use at most 192 MiB of HBM per device.

v0:
```python
import functools

import jax
import jax.numpy as jnp
from jax import lax
from jax.experimental import pallas as pl
from jax.experimental.pallas import tpu as pltpu
from jax.sharding import PartitionSpec as P

BANDS = 5
COMPONENTS = 12
PARAMS = 44
PATCH = 64
TAPS = 25
HALF = TAPS // 2
TILE_COLS = 8
TILE_SIDE = 384
QUAD = TILE_SIDE // 2
SRC = 8
TILES = 64
N_BAND = 4
PARTNERS = 16
SLOTS = PARTNERS * SRC
LANES = 128

TOP, LEFT, LIVE = 8, 9, 10
WEIGHT, SPREAD_Y, SPREAD_X = 16, 32, 48
HALVES = 64

PER_CHUNK = 21
COLS = 256
CHUNKS = -(-SLOTS // PER_CHUNK)
SPAN = 224
GROUP = 48
STEP = 80
HALF_SPAN = SPAN // 2
BACK_START = QUAD - HALF_SPAN

flux_scale = 2.0
prior_weight = 0.1
highest = lax.Precision.HIGHEST
f32 = jnp.float32
bf16 = jnp.bfloat16
MESH = pl.DeviceIdType.MESH


def iota(shape, axis):
    return lax.broadcasted_iota(jnp.int32, shape, axis)


def dot(a, b, dims=((1,), (0,)), precision=None):
    return lax.dot_general(a, b, (dims, ((), ())), precision=precision, preferred_element_type=f32)


def halves(x):
    high = x.astype(bf16)
    return high, (x - high.astype(f32)).astype(bf16)


def dot3(a, b, dims=((1,), (0,))):
    rows = a.shape[0] // 2
    both = dot(a, b[0], dims)
    return both[:rows] + (both[rows:] + dot(a[:rows], b[1], dims))


def wrapped_tile(row, col):
    return lax.rem(row + TILE_COLS, TILE_COLS) * TILE_COLS + lax.rem(col + TILE_COLS, TILE_COLS)


def inside(row, col):
    return (row >= 0) & (row < TILE_COLS) & (col >= 0) & (col < TILE_COLS)


def viewers(tile, band):
    home = lax.rem(tile + TILES // 2, TILES)
    row, col = home // TILE_COLS, lax.rem(home, TILE_COLS)
    found = []
    for step_y, half_y in ((1, 0), (-1, 1), (0, 0), (0, 1)):
        for step_x, half_x in ((1, 0), (-1, 1), (0, 0), (0, 1)):
            far = 2 * abs(step_y) + abs(step_x)
            answer = (2 * abs(step_y) + half_y) * 4 + 2 * abs(step_x) + half_x
            to_row, to_col = row + step_y, col + step_x
            found.append(
                (
                    wrapped_tile(to_row, to_col),
                    2 * half_y + half_x,
                    far * N_BAND + band,
                    answer,
                    inside(to_row, to_col),
                )
            )
    return found


def owners(tile, band):
    row, col = tile // TILE_COLS, lax.rem(tile, TILE_COLS)
    half_y, half_x = band // 2, lax.rem(band, 2)
    found = []
    for far_y in (1, 0):
        for far_x in (1, 0):
            from_row, from_col = row + far_y * (2 * half_y - 1), col + far_x * (2 * half_x - 1)
            holder = lax.rem(wrapped_tile(from_row, from_col) + TILES // 2, TILES)
            answer = (2 * far_y + half_y) * 4 + 2 * far_x + half_x
            for other in range(N_BAND):
                block = (2 * far_y + far_x) * N_BAND + other
                found.append((holder, other, block, answer, inside(from_row, from_col)))
    return found


def greet(barrier, callers):
    for other_tile, other_band, _, _, there in callers:

        @pl.when(there)
        def _():
            pl.semaphore_signal(
                barrier, inc=1, device_id=(other_tile, other_band), device_id_type=MESH
            )


def how_many(partners):
    return sum(there.astype(jnp.int32) for _, _, _, _, there in partners)


def parameter_lanes():
    lane = iota((1, LANES), 1)
    source = jnp.where(lane < BANDS + 2, lane, -1)
    source = jnp.where(lane == BANDS + 2, PARAMS - 1, source)
    for j, base in enumerate((WEIGHT, SPREAD_Y, SPREAD_X)):
        here = (lane >= base) & (lane < base + COMPONENTS)
        source = jnp.where(here, BANDS + 2 + 3 * (lane - base) + j, source)
    return (iota((PARAMS, LANES), 0) == source).astype(bf16)


def parameter_columns():
    lane = iota((LANES, LANES), 0)
    target = jnp.where(lane < BANDS + 2, lane, -1)
    target = jnp.where(lane == BANDS + 2, PARAMS - 1, target)
    for j, base in enumerate((WEIGHT, SPREAD_Y, SPREAD_X)):
        here = (lane >= base) & (lane < base + COMPONENTS)
        target = jnp.where(here, BANDS + 2 + 3 * (lane - base) + j, target)
    return (iota((LANES, LANES), 1) == target).astype(bf16)


def thirds_of(x):
    high, low = halves(x)
    return jnp.concatenate([high, low, (x - high.astype(f32) - low.astype(f32)).astype(bf16)], axis=0)


def summed(x):
    rows = x.shape[0] // 3
    return x[:rows] + (x[rows : 2 * rows] + x[2 * rows :])


def derived(params):
    raw = summed(dot(thirds_of(params), parameter_lanes()))
    lane = iota(raw.shape, 1)
    is_flux = lane < BANDS
    is_shift = (lane >= BANDS) & (lane < BANDS + 2)
    is_weight = (lane >= WEIGHT) & (lane < WEIGHT + COMPONENTS)
    is_spread = ((lane >= SPREAD_Y) & (lane < SPREAD_Y + COMPONENTS)) | (
        (lane >= SPREAD_X) & (lane < SPREAD_X + COMPONENTS)
    )
    most = jnp.max(jnp.where(is_weight, raw, -jnp.inf), axis=1, keepdims=True)
    power = jnp.where(is_weight, jnp.exp(jnp.where(is_weight, raw - most, 0.0)), 0.0)
    weight = power / jnp.sum(power, axis=1, keepdims=True)
    decay = jnp.exp(-jnp.abs(raw))
    soft = jnp.maximum(raw, 0.0) + jnp.log1p(decay)
    sigmoid = jnp.where(raw >= 0.0, 1.0, decay) / (1.0 + decay)
    curve = jnp.tanh(raw)
    softness = jnp.exp(0.25 * raw[:, BANDS + 2 : BANDS + 3])
    scale = (PATCH / 32.0) * softness
    spread = (0.5 + soft) * scale
    return raw, is_flux, is_shift, is_weight, is_spread, weight, soft, sigmoid, curve, scale, spread


def start_copies(pairs, sems):
    copies = [pltpu.make_async_copy(src, dst, sems.at[i]) for i, (src, dst) in enumerate(pairs)]
    for copy in copies:
        copy.start()
    return copies


def build_tables(taps, conv, back):
    tap, spot = iota((TAPS, COLS), 0), iota((TAPS, COLS), 1)

    def spread_out(x, places):
        return dot(x, (places == spot).astype(bf16))

    def turned(row, rows, shift):
        wide = jnp.broadcast_to(row, (rows, COLS))
        return pltpu.roll(wide, shift, 1, stride=1, stride_axis=0)

    lane = iota((HALF_SPAN, COLS), 1)
    for side in range(2):
        high, low = halves(taps[side])
        ahead = spread_out(high, tap) + spread_out(high, tap + STEP) + spread_out(low, tap + 2 * STEP)
        behind = [spread_out(half, lax.rem(COLS - tap, COLS)) for half in (high, low)]
        for b in range(BANDS):
            conv[side, b * GROUP : (b + 1) * GROUP, :] = turned(ahead[b : b + 1], GROUP, 0).astype(bf16)
            for part in range(2):
                shift = (HALF_SPAN - BACK_START) * part
                near = turned(behind[0][b : b + 1], HALF_SPAN, shift)
                far = turned(behind[0][b : b + 1], HALF_SPAN, shift + HALF_SPAN)
                small = turned(behind[1][b : b + 1], HALF_SPAN, shift)
                both = jnp.where(lane < HALF_SPAN, near, jnp.where(lane < SPAN, far, 0.0))
                small = jnp.where(lane < HALF_SPAN, small, 0.0)
                cols = slice(b * COLS, (b + 1) * COLS)
                back[side, part, :HALF_SPAN, cols] = both.astype(bf16)
                back[side, part, HALF_SPAN:, cols] = small.astype(bf16)


def send_kernel(
    params,
    offsets,
    counts,
    psf_y,
    psf_x,
    background,
    image,
    out,
    conv,
    back,
    prior,
    sky,
    observed,
    theta,
    place,
    taps,
    pixels,
    mine,
    landed,
    load_sem,
    send_sem,
    recv_sem,
):
    tile, band = lax.axis_index("tile"), lax.axis_index("band")
    loads = start_copies(
        (
            (params, theta),
            (offsets, place),
            (psf_y, taps.at[0]),
            (psf_x, taps.at[1]),
            (background, sky),
            (quadrant_of(image, tile, band), pixels),
        ),
        load_sem,
    )
    barrier = pltpu.get_barrier_semaphore()
    greet(barrier, owners(tile, band))
    for load in loads[:2]:
        load.wait()
    raw, is_flux, is_shift, is_weight, is_spread, weight, soft, sigmoid, curve, scale, spread = derived(
        theta[...]
    )
    slot, lane = iota((SRC, LANES), 0), iota((SRC, LANES), 1)
    live = (slot < counts[0]).astype(f32)
    row = jnp.where(is_flux, flux_scale * soft * live, 0.0)
    row = jnp.where(is_shift, (PATCH / 16.0) * curve, row)
    row = jnp.where(is_weight, weight, row)
    row = jnp.where(is_spread, spread, row)
    start = place[...].astype(f32)
    diagonal = iota((SRC, SRC), 0) == iota((SRC, SRC), 1)
    for side in range(2):
        start_side = jnp.sum(jnp.where(diagonal, start[side : side + 1, :], 0.0), axis=1, keepdims=True)
        row = jnp.where(lane == TOP + side, start_side, row)
    row = jnp.where(lane == LIVE, live, row)
    slope = jnp.where(is_flux, sigmoid / soft, 0.0)
    slope = jnp.where(is_shift, (PATCH / 16.0) * (1.0 - curve * curve), slope)
    slope = jnp.where(is_weight, 1.0, slope)
    slope = jnp.where(is_spread, scale * sigmoid, slope)
    mine[...] = row + pltpu.roll(slope, HALVES, 1)

    pl.semaphore_wait(barrier, how_many(viewers(tile, band)))
    copies = []
    for i, (other_tile, other_band, block, _, there) in enumerate(viewers(tile, band)):
        copy = pltpu.make_async_remote_copy(
            src_ref=mine,
            dst_ref=landed.at[block],
            send_sem=send_sem.at[i],
            recv_sem=recv_sem.at[block],
            device_id=(other_tile, other_band),
            device_id_type=MESH,
        )
        copies.append((copy, there))
        pl.when(there)(copy.start)
    for _, _, block, _, there in owners(tile, band):

        @pl.when(jnp.logical_not(there))
        def _():
            landed[block] = jnp.zeros((SRC, LANES), f32)

    for load in loads[2:]:
        load.wait()
    build_tables(taps, conv, back)

    prior[...] = prior_weight * theta[...] * live[:, :PARAMS]
    turn = lax.rem(COLS - lax.rem(band, 2) * (QUAD - COLS // 2), COLS)
    for b in range(BANDS):
        observed[b] = pltpu.roll(pixels[b], turn, 1)[:, :QUAD]

    for i, (other_tile, other_band, block, _, there) in enumerate(reversed(owners(tile, band))):
        copy = pltpu.make_async_remote_copy(
            src_ref=mine,
            dst_ref=landed.at[block],
            send_sem=send_sem.at[i],
            recv_sem=recv_sem.at[block],
            device_id=(other_tile, other_band),
            device_id_type=MESH,
        )
        pl.when(there)(copy.wait_recv)
        out[block * SRC : (block + 1) * SRC, :] = landed[block]
    for copy, there in copies:
        pl.when(there)(copy.wait_send)


def quadrant_of(image, tile, band):
    half_y, half_x = band // 2, lax.rem(band, 2)
    rows = pl.ds(pl.multiple_of(half_y * QUAD, QUAD), QUAD)
    cols = pl.ds(pl.multiple_of(half_x * (COLS // 2), COLS // 2), COLS)
    return image.at[0, :, rows, cols]


def column_comps():
    column = iota((1, COLS), 1)
    place = (column * 5462) >> 16
    return place, iota((16, COLS), 0) == column - COMPONENTS * place


def one_of(values, base):
    mine = column_comps()[1]
    return jnp.sum(jnp.where(mine, values[base : base + 16], 0.0), axis=0, keepdims=True)


def geometry(values, side):
    spread = one_of(values, (SPREAD_Y, SPREAD_X)[side])
    inverse = 1.0 / jnp.where(spread > 0.0, spread, 1.0)
    shift = values[BANDS + side : BANDS + side + 1]
    start = values[TOP + side : TOP + side + 1]
    spot = iota((SPAN, COLS), 0).astype(f32) - (start + float(HALF))
    inside = (spot >= 0.0) & (spot < PATCH)
    ratio = (spot + (0.5 - PATCH / 2.0) - shift) * inverse
    spot = iota((QUAD, COLS), 0).astype(f32) - start
    window = ((spot >= 0.0) & (spot < PATCH)).astype(f32)
    return inverse, inside, ratio, window


def render(values, conv, profiles, factors, c):
    weight = one_of(values, WEIGHT)
    for side in range(2):
        _, inside, ratio, window = geometry(values, side)
        profile = jnp.where(inside, jnp.exp(-0.5 * ratio * ratio), 0.0)
        profiles[c, side] = profile
        high, low = halves(profile)
        for start in range(0, QUAD, GROUP):
            rows = slice(start, start + STEP)
            blank = jnp.zeros((COLS - 3 * STEP, COLS), bf16)
            stack = jnp.concatenate([high[rows], low[rows], high[rows], blank], axis=0)
            factor = dot(conv[side], stack)
            seen = window[start : start + GROUP]
            for b in range(BANDS):
                scale = seen * (weight * values[b : b + 1]) if side == 0 else seen
                high_low = halves(factor[b * GROUP : (b + 1) * GROUP] * scale)
                for half in range(2):
                    put = half * QUAD + start
                    factors[side][c, b, put : put + GROUP] = high_low[half]


def model_of(factors, c, b):
    y_factor, x_factor = factors
    x = (x_factor[c, b, :QUAD], x_factor[c, b, QUAD:])
    return dot3(y_factor[c, b], x, ((1,), (1,)))


def leave(observed, background, model, residual, b):
    left = observed[b] / (background[0:1, b : b + 1] + model) - 1.0
    left = left * (1.0 / (PATCH * PATCH))
    for way, r in enumerate((left, left.T)):
        high_low = halves(r)
        for half in range(2):
            residual[way, b, half * QUAD : (half + 1) * QUAD] = high_low[half]


def pull(values, onehot, back, profiles, factors, residual, stack, c):
    y_factor, x_factor = factors
    mine = column_comps()[1]
    weight = one_of(values, WEIGHT)
    rows = []
    inverse_y, _, ratio_y, window_y = geometry(values, 0)
    inverse_x, _, ratio_x, window_x = geometry(values, 1)
    blank = jnp.zeros((COLS - SPAN, COLS), bf16)
    for b in range(BANDS):
        y = (y_factor[c, b, :QUAD], y_factor[c, b, QUAD:])
        x = (x_factor[c, b, :QUAD], x_factor[c, b, QUAD:])
        along_y = dot3(residual[0, b], x)
        along_x = dot3(residual[1, b], y)
        factor = y[0].astype(f32) + y[1].astype(f32)
        rows.append(jnp.sum(along_y * factor, axis=0, keepdims=True))
        along_y = along_y * (window_y * (weight * values[b : b + 1]))
        along_x = along_x * window_x
        for side, along in enumerate((along_y, along_x)):
            high, low = halves(along)
            for part, start in enumerate((0, BACK_START)):
                here = slice(start, start + HALF_SPAN)
                put = b * COLS
                stack[side, part, put : put + HALF_SPAN] = high[here]
                stack[side, part, put + HALF_SPAN : put + SPAN] = low[here]
                stack[side, part, put + SPAN : put + COLS] = blank
    ds = []
    for side in range(2):
        d = []
        for part in range(2):
            both = dot(back[side, part], stack[side, part])
            d.append(both[:HALF_SPAN] + both[HALF_SPAN:])
        ds.append(jnp.concatenate(d, axis=0))
    by_comp = rows[0] + rows[1] + rows[2] + rows[3] + rows[4]
    spreads = []
    for side, (d, inverse, ratio) in enumerate(((ds[0], inverse_y, ratio_y), (ds[1], inverse_x, ratio_x))):
        first = d * profiles[c, side] * ratio
        rows.append(inverse * jnp.sum(first, axis=0, keepdims=True))
        spreads.append(inverse * jnp.sum(first * ratio, axis=0, keepdims=True))
    pieces = rows + [jnp.zeros((16 - len(rows), COLS), f32)]
    for by in (by_comp, spreads[0], spreads[1]):
        pieces.append(jnp.where(mine, by, 0.0))
    high_low = jnp.concatenate(halves(jnp.concatenate(pieces, axis=0)), axis=0)
    return dot(onehot, high_low, ((1,), (1,)))


def find(data, tile, band):
    row, col = tile // TILE_COLS, lax.rem(tile, TILE_COLS)
    half_y, half_x = band // 2, lax.rem(band, 2)
    slot = iota((SLOTS, LANES), 0)
    lane = iota((SLOTS, LANES), 1)
    far_y, far_x = slot // (SLOTS // 2), lax.rem(slot // (SLOTS // 4), 2)

    def moved(far, half, place):
        origin = jnp.where(far == 0, 0, TILE_SIDE * (2 * half - 1)) - QUAD * half
        beyond = place + 2 * half - 1
        there = (far == 0) | ((beyond >= 0) & (beyond < TILE_COLS))
        return origin.astype(f32), there

    origin_y, there_y = moved(far_y, half_y, row)
    origin_x, there_x = moved(far_x, half_x, col)
    data = data + jnp.where(lane == TOP, origin_y, jnp.where(lane == LEFT, origin_x, 0.0))
    is_place = (lane == TOP) | (lane == LEFT)
    reach = is_place & (data > -PATCH) & (data < QUAD) | (lane == LIVE) & (data > 0.0)
    met = jnp.where(reach & there_y & there_x, 1.0, 0.0).astype(bf16)
    active = jnp.where(dot(met, jnp.ones((LANES, LANES), bf16)) > 2.5, 1.0, 0.0)
    count = jnp.sum(active, axis=0, keepdims=True)

    def chunk_makers():
        before = jnp.where(lane < slot, 1.0, 0.0).astype(bf16)
        order = dot(before, active.astype(bf16))
        order = jnp.where(active > 0.0, order, -1.0)[:, 0:1].astype(jnp.int32)
        place = column_comps()[0]

        def picked(c):
            here = (place < PER_CHUNK) & (order - c * PER_CHUNK == place)
            return jnp.where(here, 1.0, 0.0).astype(bf16)

        thirds = thirds_of(data.T[:HALVES])

        def gathered(c):
            return summed(dot(thirds, picked(c)))

        return picked, gathered

    return count, chunk_makers


def more_kernel(
    slots,
    sky,
    observed,
    conv,
    back,
    rest_model,
    rest_parts,
    profiles,
    y_factor,
    x_factor,
    residual,
    stack,
):
    tile, band = lax.axis_index("tile"), lax.axis_index("band")
    counts, chunk_makers = find(slots[...], tile, band)
    count = counts[0, 0].astype(jnp.int32)

    @pl.when(count > PER_CHUNK)
    def _():
        picked, gathered = chunk_makers()
        factors = (y_factor, x_factor)
        chunks = (count + PER_CHUNK - 1) // PER_CHUNK
        rest_model[...] = jnp.zeros_like(rest_model)
        rest_parts[...] = jnp.zeros_like(rest_parts)

        def add(c, carry):
            render(gathered(c), conv, profiles, factors, c)
            for b in range(BANDS):
                rest_model[b] += model_of(factors, c, b)
            return carry

        lax.fori_loop(1, chunks, add, 0)
        render(gathered(0), conv, profiles, factors, 0)
        for b in range(BANDS):
            model = rest_model[b] + model_of(factors, 0, b)
            leave(observed, sky, model, residual, b)

        def take(c, carry):
            rest_parts[...] += pull(gathered(c), picked(c), back, profiles, factors, residual, stack, c)
            return carry

        lax.fori_loop(1, chunks, take, 0)


def to_parameters(pulled, data):
    lane = iota((SLOTS, LANES), 1)
    is_weight = (lane >= WEIGHT) & (lane < WEIGHT + COMPONENTS)
    is_spread = ((lane >= SPREAD_Y) & (lane < SPREAD_Y + COMPONENTS)) | (
        (lane >= SPREAD_X) & (lane < SPREAD_X + COMPONENTS)
    )
    weight = jnp.where(is_weight, data, 0.0)
    groups = jnp.concatenate(
        [jnp.where(is_weight, pulled, 0.0), jnp.where(is_spread, pulled * data, 0.0)], axis=0
    )
    sums = summed(dot(thirds_of(groups), jnp.ones((LANES, LANES), bf16)))
    slope = jnp.where(lane < HALVES, pltpu.roll(data, HALVES, 1), 0.0)
    by_lane = pulled * slope - weight * sums[:SLOTS]
    by_lane = jnp.where(lane == BANDS + 2, 0.25 * sums[SLOTS:], by_lane)
    return summed(dot(thirds_of(by_lane), parameter_columns()))


def return_kernel(
    slots,
    rest_model,
    rest_parts,
    sky,
    observed,
    conv,
    back,
    prior,
    out,
    profiles,
    y_factor,
    x_factor,
    residual,
    stack,
    parts,
    landed,
    send_sem,
    recv_sem,
):
    tile, band = lax.axis_index("tile"), lax.axis_index("band")
    barrier = pltpu.get_barrier_semaphore()
    greet(barrier, viewers(tile, band))
    factors = (y_factor, x_factor)
    count, chunk_makers = find(slots[...], tile, band)
    picked, gathered = chunk_makers()
    onehot, values = picked(0), gathered(0)
    more = count[:, 0:1] > PER_CHUNK
    render(values, conv, profiles, factors, 0)
    for b in range(BANDS):
        model = model_of(factors, 0, b) + jnp.where(more, rest_model[b], 0.0)
        leave(observed, sky, model, residual, b)
    pulled = pull(values, onehot, back, profiles, factors, residual, stack, 0)
    pulled = pulled + jnp.where(more, rest_parts[...], 0.0)
    parts[...] = to_parameters(pulled + pltpu.roll(pulled, HALVES, 1), slots[...])

    pl.semaphore_wait(barrier, how_many(owners(tile, band)))
    copies = []
    for i, (other_tile, other_band, block, answer, there) in enumerate(owners(tile, band)):
        copy = pltpu.make_async_remote_copy(
            src_ref=parts.at[block * SRC : (block + 1) * SRC, :],
            dst_ref=landed.at[answer],
            send_sem=send_sem.at[i],
            recv_sem=recv_sem.at[answer],
            device_id=(other_tile, other_band),
            device_id_type=MESH,
        )
        copies.append((copy, there))
        pl.when(there)(copy.start)
    for _, _, _, answer, there in viewers(tile, band):

        @pl.when(jnp.logical_not(there))
        def _():
            landed[answer] = jnp.zeros((SRC, LANES), f32)

    total = jnp.zeros((SRC, LANES), f32)
    for i, (other_tile, other_band, _, answer, there) in enumerate(reversed(viewers(tile, band))):
        copy = pltpu.make_async_remote_copy(
            src_ref=parts.at[0:SRC, :],
            dst_ref=landed.at[answer],
            send_sem=send_sem.at[i],
            recv_sem=recv_sem.at[answer],
            device_id=(other_tile, other_band),
            device_id_type=MESH,
        )
        pl.when(there)(copy.wait_recv)
        total = total + landed[answer]
    out[...] = total[:, :PARAMS] - prior[...]
    for copy, there in copies:
        pl.when(there)(copy.wait_send)


def vmem(count):
    return [pl.BlockSpec(memory_space=pltpu.VMEM)] * count


def hbm(count):
    return [pl.BlockSpec(memory_space=pltpu.HBM)] * count


def work_space(chunks):
    return [
        pltpu.VMEM((chunks, 2, SPAN, COLS), f32),
        pltpu.VMEM((chunks, BANDS, 2 * QUAD, COLS), bf16),
        pltpu.VMEM((chunks, BANDS, 2 * QUAD, COLS), bf16),
        pltpu.VMEM((2, BANDS, 2 * QUAD, QUAD), bf16),
        pltpu.VMEM((2, 2, BANDS * COLS, COLS), bf16),
    ]


def shape(*dims, kind=f32):
    return jax.ShapeDtypeStruct(dims, kind)


def body(params, offsets, counts, image, background, psf_y, psf_x):
    smem = pl.BlockSpec(memory_space=pltpu.SMEM)
    params, offsets, image, background, psf_y, psf_x = (
        pltpu.with_memory_space_constraint(x, pltpu.HBM)
        for x in (params, offsets.T, image, background, psf_y, psf_x)
    )
    partners = [pltpu.SemaphoreType.DMA((PARTNERS,))] * 2
    slots, conv, back, prior, sky, observed = pl.pallas_call(
        send_kernel,
        out_shape=[shape(SLOTS, LANES)]
        + [shape(2, BANDS * GROUP, COLS, kind=bf16), shape(2, 2, SPAN, BANDS * COLS, kind=bf16)]
        + [shape(SRC, PARAMS), shape(1, BANDS), shape(BANDS, QUAD, QUAD)],
        in_specs=hbm(2) + [smem] + hbm(4),
        out_specs=vmem(6),
        scratch_shapes=[
            pltpu.VMEM((SRC, PARAMS), f32),
            pltpu.VMEM((2, SRC), jnp.int32),
            pltpu.VMEM((2, BANDS, TAPS), f32),
            pltpu.VMEM((BANDS, QUAD, COLS), f32),
            pltpu.VMEM((SRC, LANES), f32),
            pltpu.VMEM((PARTNERS, SRC, LANES), f32),
            pltpu.SemaphoreType.DMA((6,)),
        ]
        + partners,
        compiler_params=pltpu.CompilerParams(
            collective_id=0, has_side_effects=True, vmem_limit_bytes=16 * 1024 * 1024
        ),
        name="send_slots",
    )(params, offsets, counts, psf_y, psf_x, background, image)
    rest_model, rest_parts = pl.pallas_call(
        more_kernel,
        out_shape=[shape(BANDS, QUAD, QUAD), shape(SLOTS, LANES)],
        in_specs=vmem(5),
        out_specs=vmem(2),
        scratch_shapes=work_space(CHUNKS),
        compiler_params=pltpu.CompilerParams(vmem_limit_bytes=40 * 1024 * 1024),
        name="more_sources",
    )(slots, sky, observed, conv, back)
    return pl.pallas_call(
        return_kernel,
        out_shape=shape(SRC, PARAMS),
        in_specs=vmem(8),
        out_specs=vmem(1)[0],
        scratch_shapes=work_space(1)
        + [
            pltpu.VMEM((SLOTS, LANES), f32),
            pltpu.VMEM((PARTNERS, SRC, LANES), f32),
        ]
        + partners,
        compiler_params=pltpu.CompilerParams(
            collective_id=1, has_side_effects=True, vmem_limit_bytes=24 * 1024 * 1024
        ),
        name="return_parts",
    )(
        slots, rest_model, rest_parts, sky, observed, conv, back, prior
    )


def solution(mesh):
    placed = (
        P(("tile", "band"), None),
        P(("tile", "band"), None),
        P(("tile", "band")),
        P("tile", None, None, None),
        P("tile", None),
        P(),
        P(),
    )
    return jax.shard_map(
        body, mesh=mesh, in_specs=placed, out_specs=P(("tile", "band"), None), check_vma=False
    )
```

profile of v0, /device:TPU:1, one launch (start us, length us, event | category | flops | bytes accessed | tf_op | source)
XLA Modules:
  0.0 32.2 jit_solution(1731279399992831247)
XLA Ops:
  0.7 16.2 %send_slots.1 = (f32[128,128]{1,0:T(8,128)S(1)}, bf16[2,240,256]{2,1,0:T(8,128)(2,1)S(1)}, bf16[2,2,224,1280]{3,2,1,0:T(8,128)(2,1)S(1)}, f32[8,44]{1,0:T(8,128)...) custom-call(f32[8,44]{1,0:T(8,128)} %params.1, s32[2,8]{1,0:T(2,128)} %bitcast.1, s32[1]{0:T(128)S(6)} %copy.9.counts, ...), custom_call_target="tpu_custom_call" | custom-call | tf_op jit(solution)/shard_map/send_slots/pallas_call | solution.py:633
  16.9 0.2 more_sources.1
  17.1 14.4 %return_parts.1 = f32[8,44]{1,0:T(8,128)S(1)} custom-call(f32[128,128]{1,0:T(8,128)S(1)} %get-tuple-element.13.slots, f32[5,192,192]{2,1,0:T(8,128)S(1)} %get-tuple-element.18.rest_model, f32[128,128]{1,0:T(8,128)S(1)} %get-tuple-element.19.rest_parts, f32[1,5]{1,0:T(1,128)S(1)} %get-tuple-element.14.sky, f32[5,192,192]{2,1,0:T(8,128)S(1)} %get-tuple-element.15.observed, ...), custom_call_target="tpu_custom_call" | custom-call | tf_op jit(solution)/shard_map/return_parts/pallas_call | solution.py:664
  31.6 0.6 %copy.10 = f32[8,44]{1,0:T(8,128)} copy(f32[8,44]{1,0:T(8,128)S(1)} %return_parts.1) | data formatting | bytes 2816
where the time goes:
time: 32.3 us; the launch traced here: 32.2 us
  Pallas kernels  30.9 us (96%)
  between operations  0.68 us (2%)
  local copies, waits for them, and re-layouts  0.6 us (2%)
    pallas_call x1, Pallas kernels, body(): pl.pallas_call(send_kernel, out_shape=[shape(SLOTS, LANES)] + [shape(2, B...  16.2 us
    pallas_call x1, Pallas kernels, body(): pl.pallas_call(return_kernel, out_shape=shape(SRC, PARAMS), in_specs=vmem...  14.4 us

commit v1 on v0

--- a/solution.py
+++ b/solution.py
@@ -142,8 +142,9 @@
 
 
 def thirds_of(x):
-    high, low = halves(x)
-    return jnp.concatenate([high, low, (x - high.astype(f32) - low.astype(f32)).astype(bf16)], axis=0)
+    high = x.astype(bf16).astype(f32)
+    low = (x - high).astype(bf16).astype(f32)
+    return jnp.concatenate([high, low, x - high - low], axis=0).astype(bf16)
 
 
 def summed(x):
@@ -234,6 +235,8 @@
     recv_sem,
 ):
     tile, band = lax.axis_index("tile"), lax.axis_index("band")
+    barrier = pltpu.get_barrier_semaphore()
+    greet(barrier, owners(tile, band))
     loads = start_copies(
         (
             (params, theta),
@@ -245,8 +248,6 @@
         ),
         load_sem,
     )
-    barrier = pltpu.get_barrier_semaphore()
-    greet(barrier, owners(tile, band))
     for load in loads[:2]:
         load.wait()
     raw, is_flux, is_shift, is_weight, is_spread, weight, soft, sigmoid, curve, scale, spread = derived(

time: 32.3 us -> 32.3 us (level)
  no operation moved by 1% of the time
where the time goes in v1:
time: 32.3 us; the launch traced here: 32.2 us
  Pallas kernels  30.9 us (96%)
  between operations  0.68 us (2%)
  local copies, waits for them, and re-layouts  0.6 us (2%)
    pallas_call x1, Pallas kernels, body(): pl.pallas_call(send_kernel, out_shape=[shape(SLOTS, LANES)] + [shape(2, B...  16.2 us
    pallas_call x1, Pallas kernels, body(): pl.pallas_call(return_kernel, out_shape=shape(SRC, PARAMS), in_specs=vmem...  14.4 us

profile of v1, /device:TPU:1, one launch (start us, length us, event | category | flops | bytes accessed | tf_op | source)
XLA Modules:
  0.0 32.2 jit_solution(17092309833722186252)
XLA Ops:
  0.7 16.2 %send_slots.1 = (f32[128,128]{1,0:T(8,128)S(1)}, bf16[2,240,256]{2,1,0:T(8,128)(2,1)S(1)}, bf16[2,2,224,1280]{3,2,1,0:T(8,128)(2,1)S(1)}, f32[8,44]{1,0:T(8,128)...) custom-call(f32[8,44]{1,0:T(8,128)} %params.1, s32[2,8]{1,0:T(2,128)} %bitcast.1, s32[1]{0:T(128)S(6)} %copy.9.counts, ...), custom_call_target="tpu_custom_call" | custom-call | tf_op jit(solution)/shard_map/send_slots/pallas_call | solution.py:634
  16.9 0.2 more_sources.1
  17.1 14.4 %return_parts.1 = f32[8,44]{1,0:T(8,128)S(1)} custom-call(f32[128,128]{1,0:T(8,128)S(1)} %get-tuple-element.13.slots, f32[5,192,192]{2,1,0:T(8,128)S(1)} %get-tuple-element.18.rest_model, f32[128,128]{1,0:T(8,128)S(1)} %get-tuple-element.19.rest_parts, f32[1,5]{1,0:T(1,128)S(1)} %get-tuple-element.14.sky, f32[5,192,192]{2,1,0:T(8,128)S(1)} %get-tuple-element.15.observed, ...), custom_call_target="tpu_custom_call" | custom-call | tf_op jit(solution)/shard_map/return_parts/pallas_call | solution.py:665
  31.6 0.6 %copy.10 = f32[8,44]{1,0:T(8,128)} copy(f32[8,44]{1,0:T(8,128)S(1)} %return_parts.1) | data formatting | bytes 2816
